TPU v7x, 256 devices: a whole 4x4x8 slice. The times are simulated.
256 devices in a mesh: expert: 64 (over z, y, core), tensor: 4 (over x).
Axes of the slice: x: 4, y: 4, z: 8, core: 2. Of those that a mesh axis runs over, the one named last changes fastest.
Arguments:
- tokens: bfloat16 [8192, 4096], P('expert'), may hold values from -6 to 6
- routing: int32 [8192, 8], P('expert'), may hold values from 0 to 63, all different within a row; in each aligned block of 128 rows (0 to 127, 128 to 255, ...) at most 20 rows name the same one
- gate_weights: float32 [8192, 8], P('expert'), may hold values from 0.05 to 0.45
- w_gate: bfloat16 [64, 4096, 1536], P('expert', None, 'tensor'), may hold values from -0.09375 to 0.09375
- w_up: bfloat16 [64, 4096, 1536], P('expert', None, 'tensor'), may hold values from -0.09375 to 0.09375
- w_down: bfloat16 [64, 1536, 4096], P('expert', 'tensor'), may hold values from -0.15625 to 0.15625
Outputs:
- mixed: bfloat16 [8192, 4096], P('expert', 'tensor')
Inputs may be any that keep to these rules, and one draw needn't show every extreme that they name: `routing`: within the rows of one device (128 tokens) a token never names an expert twice, and no expert is named more than 20 times; in every draw some expert is named exactly 20 times in the rows of some device.
All inputs are finite; a program needn't handle non-finite values.
Results may differ from a plain program's by a relative error of at most 0.015.
Values may be sent and summed in bfloat16 or wider, within the bound.
A program may use at most 128 MiB of HBM per device.

v0:
```python
import jax
import jax.numpy as jnp
from jax import lax
from jax.sharding import PartitionSpec as P


def local(tokens, routing, gate_weights, w_gate, w_up, w_down):
    tok_rows, top_count = routing.shape
    features = tokens.shape[1]
    groups = lax.axis_size("expert")
    experts = groups * w_gate.shape[0]
    capacity = min(tok_rows, max(2, tok_rows * top_count * 5 // (4 * experts)))
    routes_flat = routing.reshape(-1)
    onehot = (routes_flat[:, None] == jnp.arange(experts, dtype=jnp.int32)[None, :]).astype(
        jnp.int32
    )
    earlier = jnp.cumsum(onehot, axis=0) - onehot
    slot_index = jnp.sum(earlier * onehot, axis=1)
    target = routes_flat * capacity + slot_index
    source = jnp.arange(tok_rows * top_count, dtype=jnp.int32) // top_count
    owners = jnp.zeros((experts * capacity,), jnp.int32).at[target].set(source)
    filled = (
        jnp.zeros((experts * capacity,), jnp.bfloat16)
        .at[target]
        .set(jnp.ones((tok_rows * top_count,), jnp.bfloat16))
    )
    outgoing = (tokens[owners] * filled[:, None]).reshape(experts, capacity, features)
    arrived = lax.all_to_all(outgoing, "expert", split_axis=0, concat_axis=0, tiled=True)
    rows_in = arrived.reshape(-1, features)
    gate_proj = jnp.dot(rows_in, w_gate[0], preferred_element_type=jnp.float32)
    up_proj = jnp.dot(rows_in, w_up[0], preferred_element_type=jnp.float32)
    hidden = (jax.nn.silu(gate_proj) * up_proj).astype(jnp.bfloat16)
    partial_term = jnp.dot(hidden, w_down[0], preferred_element_type=jnp.float32)
    summed = lax.psum_scatter(
        partial_term.astype(jnp.bfloat16), "tensor", scatter_dimension=1, tiled=True
    ).astype(jnp.float32)
    returned = lax.all_to_all(
        summed.reshape(experts, capacity, -1).astype(jnp.bfloat16),
        "expert",
        split_axis=0,
        concat_axis=0,
        tiled=True,
    ).astype(jnp.float32)
    picked = returned.reshape(experts * capacity, -1)[target].reshape(tok_rows, top_count, -1)
    combined = jnp.zeros((tok_rows, picked.shape[2]), jnp.float32)
    for position in range(top_count):
        combined = combined + gate_weights[:, position : position + 1] * picked[:, position]
    return combined.astype(jnp.bfloat16)


def solution(mesh):
    return jax.shard_map(
        local,
        mesh=mesh,
        in_specs=(
            P("expert", None),
            P("expert", None),
            P("expert", None),
            P("expert", None, "tensor"),
            P("expert", None, "tensor"),
            P("expert", "tensor", None),
        ),
        out_specs=P("expert", "tensor"),
        check_vma=False,
    )
```

profile of v0, /device:TPU:8, one launch (start us, length us, event | category | flops | bytes accessed | tf_op | source)
XLA Modules:
  0.0 652.2 jit_solution(12253290783731891197)
XLA Ops:
  6.5 0.9 copy.16
  8.4 0.7 fusion.34
  9.1 31.1 %reduce-window.6 = s32[64,8,128]{2,1,0:T(8,128)S(1)} reduce-window(s32[64,8,128]{2,1,0:T(8,128)} %fusion.34, s32[]{:T(128)} %constant.27.clone.1), window={size=1x1x128 pad=0_0x0_0x127_0}, to_apply=%region_0.0 | reduce-window | flops 8323072 | bytes 524292 | tf_op jit(solution)/shard_map/reduce-window
  40.2 0.8 slice.76
  41.0 1.1 copy.18
  42.2 0.8 broadcast_add_fusion
  43.3 1.0 fusion.33
  44.3 4.3 scatter_custom_fusion
  48.7 20.1 %gather_fusion = bf16[1280,4096]{1,0:T(8,128)(2,1)} fusion(bf16[128,4096]{1,0:T(8,128)(2,1)} %param.6, s32[2048]{0:T(1024)S(1)} %pad_clamp_fusion), kind=kCustom, calls=%fused_computation | custom fusion | bytes 20976640 | tf_op jit(solution)/shard_map/gather | solution.py:27
  68.7 13.9 %gather.9 = bf16[64,20,4096]{2,1,0:T(8,128)(2,1)} reshape(bf16[1280,4096]{1,0:T(8,128)(2,1)} %gather_fusion) | data formatting | bytes 20971520 | tf_op jit(solution)/shard_map/gather | solution.py:27
  82.7 7.6 %scatter_custom_fusion.1 = bf16[1280]{0:T(1024)(128)(2,1)S(1)} fusion(s32[1024]{0:T(1024)S(1)} %bitcast.119, bf16[1024]{0:T(1024)(128)(2,1)S(1)} %broadcast.65, bf16[]{:T(256)} %constant.35.clone.1), kind=kCustom, calls=%fused_computation.63 | custom fusion | bytes 2562 | tf_op jit(solution)/shard_map/scatter | solution.py:25
  90.4 6.3 broadcast_multiply_fusion
  96.7 288.0 %all_to_all.10 = bf16[64,20,4096]{2,1,0:T(8,128)(2,1)} all-to-all(bf16[64,20,4096]{2,1,0:T(8,128)(2,1)S(1)} %broadcast_multiply_fusion), channel_id=1, replica_groups=mesh['expert'=64,'tensor'=4] {'expert'}, dimensions={0} | all-to-all | bytes 20971520 | tf_op jit(solution)/shard_map/all_to_all | solution.py:28
  384.7 14.0 %reshape.69 = bf16[1280,4096]{1,0:T(8,128)(2,1)} reshape(bf16[64,20,4096]{2,1,0:T(8,128)(2,1)} %all_to_all.10) | data formatting | bytes 20971520 | tf_op jit(solution)/shard_map/reshape | solution.py:29
  398.7 10.1 %fusion.2 = f32[1280,384]{1,0:T(8,128)} fusion(bf16[1280,4096]{1,0:T(8,128)(2,1)} %reshape.69, bf16[1,4096,384]{2,1,0:T(8,128)(2,1)} %param.9), kind=kOutput, calls=%fused_computation.9 | convolution fusion | flops 4026531840 | bytes 15597568 | tf_op jit(solution)/shard_map/dot_general | solution.py:30
  408.9 17.3 %convolution_convert_fusion = bf16[1280,4096]{1,0:T(8,128)(2,1)} fusion(bf16[1,384,4096]{2,1,0:T(8,128)(2,1)S(1)} %copy-done, bf16[1280,4096]{1,0:T(8,128)(2,1)} %reshape.69, bf16[1,4096,384]{2,1,0:T(8,128)(2,1)} %param.10, f32[1280,384]{1,0:T(8,128)} %fusion.2), kind=kOutput, calls=%fused_computation.4 | convolution fusion | flops 8061255680 | bytes 29229056 | tf_op jit(solution)/shard_map/dot_general | solution.py:33
  426.2 96.4 %reduce-scatter.2.cloned.1.call-done = bf16[1280,1024]{1,0:T(8,128)(2,1)} async-done(((bf16[1280,4096]{1,0:T(8,128)(2,1)}), bf16[1280,1024]{1,0:T(8,128)(2,1)}) %reduce-scatter.2.cloned.1.call-update) | async-done | bytes 2621456 | tf_op jit(solution)/shard_map/reduce_scatter | solution.py:34
  522.6 5.2 convert_element_type.26
  527.8 10.9 %all-to-all-start.1 = ((bf16[64,20,1024]{2,1,0:T(8,128)(2,1)}), bf16[64,20,1024]{2,1,0:T(8,128)(2,1)}, u32[]{:S(2)}, u32[]{:S(2)}) async-start(bf16[64,20,1024]{2,1,0:T(8,128)(2,1)} %convert_element_type.26), calls=%async_computation.2 | async-start | bytes 6291456 | tf_op jit(solution)/shard_map/all_to_all | solution.py:37
  538.7 73.6 %all-to-all-done.1 = bf16[64,20,1024]{2,1,0:T(8,128)(2,1)} async-done(((bf16[64,20,1024]{2,1,0:T(8,128)(2,1)}), bf16[64,20,1024]{2,1,0:T(8,128)(2,1)}, u32[]{:S(2)}, u32[]{:S(2)}) %all-to-all-start.1) | async-done | bytes 2621472 | tf_op jit(solution)/shard_map/all_to_all | solution.py:37
  612.3 5.5 reshape.74
  617.8 9.0 %gather_fusion.1 = f32[1024,1024]{1,0:T(8,128)} fusion(f32[1280,1024]{1,0:T(8,128)} %reshape.74, s32[1024]{0:T(1024)S(1)} %broadcast_clamp_fusion), kind=kCustom, calls=%fused_computation.1 | custom fusion | bytes 8392704 | tf_op jit(solution)/shard_map/gather | solution.py:44
  626.8 17.2 %fusion.43 = (f32[128,1,1024]{2,1,0:T(1,128)S(1)}, f32[128,1,1024]{2,1,0:T(1,128)S(1)}, f32[128,1,1024]{2,1,0:T(1,128)S(1)}, f32[128,1,1024]{2,1,0:T(1,128)S(1)}...) fusion(f32[128,8,1024]{2,1,0:T(8,128)} %bitcast.114), kind=kLoop, calls=%fused_computation.75 | loop fusion | bytes 8388608 | tf_op jit(solution)/shard_map/slice | solution.py:47
  644.0 1.4 fusion.17
  (22 shorter events, 1.4 us)
Async XLA Ops:
  6.5 402.3 %copy-start = (bf16[1,384,4096]{2,1,0:T(8,128)(2,1)S(1)}, bf16[1,384,4096]{2,1,0:T(8,128)(2,1)}, u32[]{:S(2)}) copy-start(bf16[1,384,4096]{2,1,0:T(8,128)(2,1)} %param.11) | copy-start | bytes 9437188
  6.5 516.0 %reduce-scatter.2.cloned.1.call-start = ((), (), s32[]{:S(2)}) async-start(), calls=%async_computation.3 | async-start | bytes 13107200 | tf_op jit(solution)/shard_map/reduce_scatter | solution.py:34
  527.8 10.9 %copy-start.1 = (f32[128,8]{0,1:T(8,128)S(1)}, f32[128,8]{0,1:T(8,128)}, u32[]{:S(2)}) copy-start(f32[128,8]{0,1:T(8,128)} %param.8) | copy-start | bytes 12292
  527.8 84.5 %all-to-all-start.1 = ((bf16[64,20,1024]{2,1,0:T(8,128)(2,1)}), bf16[64,20,1024]{2,1,0:T(8,128)(2,1)}, u32[]{:S(2)}, u32[]{:S(2)}) async-start(bf16[64,20,1024]{2,1,0:T(8,128)(2,1)} %convert_element_type.26), calls=%async_computation.2 | async-start | bytes 6291456 | tf_op jit(solution)/shard_map/all_to_all | solution.py:37
Sparse Core Ops, SparseCore 0:
  426.3 96.2 reduce-scatter.1
where the time goes:
time: 655 us; the launch traced here: 652 us
  blocking collectives  288 us (44%)
  waiting for transfers between devices  170 us (26%)
  local copies, waits for them, and re-layouts  100 us (15%)
  other arithmetic  42.2 us (6%)
  matrix products  27.5 us (4%)
  between operations  13.5 us (2%)
  starting transfers between devices  10.9 us (2%)
    all_to_all x1, blocking collectives, local(): lax.all_to_all(outgoing, 'expert', split_axis=0, concat_axis=0, tiled=True)  288 us
    reduce_scatter x1, waiting for transfers between devices, local(): lax.psum_scatter(partial_term.astype(jnp.bfloat16), 'tensor', scatter_dim...  96.4 us
    all_to_all x1, waiting for transfers between devices, local(): lax.all_to_all(summed.reshape(experts, capacity, -1).astype(jnp.bfloat16)...  73.6 us
    gather x2, local copies, waits for them, and re-layouts, local(): tokens[owners] * filled[:, None]  34 us
    another operation x3, other arithmetic  32 us
    dot_general x1, matrix products, local(): jnp.dot(hidden, w_down[0], preferred_element_type=jnp.float32)  17.3 us
    slice x1, local copies, waits for them, and re-layouts, local(): picked[:, position]  17.2 us
    reshape x1, local copies, waits for them, and re-layouts, local(): rows_in = arrived.reshape(-1, features)  14 us
  transfers between devices with their start and end apart: 2, of which 2 were waited for; matrix products, arithmetic and copies ran while one was open for 0% of the time, Pallas kernels for 0%

commit v1 on v0

v1 whole, which is shorter than its diff:
```python
import functools

import jax
import jax.numpy as jnp
from jax import lax
from jax.experimental import pallas as pl
from jax.experimental.pallas import tpu as pltpu
from jax.sharding import PartitionSpec as P

MESH = pl.DeviceIdType.MESH
F32, BF16 = jnp.float32, jnp.bfloat16

NZ = 8
NP = 8
NX = 4
CAP = 20
C = 4
GR = 4 * CAP
ROWS = NP * GR
POS = {0: 0, 1: 1, 2: 2, 7: 3, 3: 4, 4: 5, 5: 6, 6: 7}


def dot(a, b):
    return jnp.dot(a, b, preferred_element_type=F32)


def kernel(tok, rt, gw, wg_h, wu_h, wd_h, out, zbuf, meta, pm, wt, yout, rows, acc, wgu, wd, hid,
           pxin, yret, zrec, fin_a, fin_s, fin_r,
           w_sem, zs, zr, ms, mr, ys, yr, yl, xs, xr, zs2, zr2, ys2, yr2, yl2, xs2, xr2, fs, fr):
    T, D = tok.shape
    Q = D // NX
    w = Q // C
    FF = hid.shape[2]
    ex = lax.axis_index("expert")
    x = lax.axis_index("tensor")
    z, p = ex // NP, ex % NP

    def zdev(step):
        return (lax.rem(z + step + NZ, NZ) * NP + p, x)

    def pdev(d):
        return (z * NP + lax.rem(p + d + NP, NP), x)

    def xdev(step):
        return (ex, lax.rem(x + step + NX, NX))

    def remote(src, dst, s, r, dev):
        return pltpu.make_async_remote_copy(src_ref=src, dst_ref=dst, send_sem=s, recv_sem=r,
                                            device_id=dev, device_id_type=MESH)

    w_copies = [
        pltpu.make_async_copy(wg_h.at[0], wgu.at[:, pl.ds(0, FF)], w_sem.at[0]),
        pltpu.make_async_copy(wu_h.at[0], wgu.at[:, pl.ds(FF, FF)], w_sem.at[1]),
        pltpu.make_async_copy(wd_h.at[0], wd, w_sem.at[2]),
    ]
    for c in w_copies:
        c.start()

    barrier = pltpu.get_barrier_semaphore()
    peers = [zdev(1), zdev(-1), xdev(1), xdev(-1)] + [pdev(d) for d in range(1, NP)]
    for dev in peers:
        pl.semaphore_signal(barrier, inc=1, device_id=dev, device_id_type=MESH)

    lane = lax.broadcasted_iota(jnp.int32, (T, 128), 1)
    sub = lax.broadcasted_iota(jnp.int32, (T, 128), 0)
    a = jnp.zeros((T, 128), F32)
    g = jnp.zeros((T, 128), F32)
    for k in range(rt.shape[1]):
        hit = rt[:, k:k + 1] == lane
        a = a + jnp.where(hit, 1.0, 0.0)
        g = g + jnp.where(hit, gw[:, k:k + 1], 0.0)
    a_t = a.T
    g_t = g.T
    earlier = jnp.where(sub < lane, 1.0, 0.0).astype(BF16)
    rank = jnp.where(a_t > 0.0, dot(a_t.astype(BF16), earlier), -64.0)
    meta[0, 0:64, :] = rank[0:64].astype(BF16)
    meta[0, 64:128, :] = g_t[0:64].astype(BF16)

    acc[...] = jnp.zeros_like(acc)
    pl.semaphore_wait(barrier, len(peers))

    def cols(r, n):
        return pl.multiple_of(lax.rem(x + r, NX) * Q + n * w, w)

    def zcopy(n, way, h):
        src, dst = (h - 1, h) if way == 0 else ((NZ - h + 1) % NZ, NZ - h)
        part = pl.ds(0, 2) if h < 4 else pl.ds(way, 1)
        return remote(zbuf.at[n, part, POS[src]], zbuf.at[n, part, POS[dst]],
                      zs.at[n, way, h - 1], zr.at[n, way, h - 1], zdev(1 if way == 0 else -1))

    def mcopy(way, h):
        src, dst = (h - 1, h) if way == 0 else ((NZ - h + 1) % NZ, NZ - h)
        return remote(meta.at[POS[src]], meta.at[POS[dst]],
                      ms.at[way, h - 1], mr.at[way, h - 1], zdev(1 if way == 0 else -1))

    def zstart(n, h):
        for way in range(2):
            zcopy(n, way, h).start()

        @pl.when(n == 0)
        def _():
            for way in range(2 if h < 4 else 1):
                mcopy(way, h).start()

    def zwait(n, h):
        for way in range(2):
            zcopy(n, way, h).wait_recv()

        @pl.when(n == 0)
        def _():
            for way in range(2 if h < 4 else 1):
                mcopy(way, h).wait_recv()

    def block(ref, n, gi, d, count=1):
        return ref.at[n, pl.ds(0, 2), gi, pl.ds(pl.multiple_of(d * GR, 16), count * GR)]

    def ystart(src, dst, s, r, loc, n, gi, sign):
        def one(d, _):
            remote(block(src, n, gi, d), block(dst, n, gi, d), s.at[n, gi], r.at[n, gi], pdev(sign * d)).start()
            return 0
        lax.fori_loop(1, NP, one, 0)
        pltpu.make_async_copy(block(src, n, gi, 0), block(dst, n, gi, 0), loc.at[n, gi]).start()

    def ywait(src, dst, s, r, loc, n, gi):
        remote(block(src, n, gi, 1, NP - 1), block(dst, n, gi, 1, NP - 1), s.at[n, gi], r.at[n, gi], pdev(1)).wait_recv()
        pltpu.make_async_copy(block(src, n, gi, 0), block(dst, n, gi, 0), loc.at[n, gi]).wait()

    def ysent(src, dst, s, r, n, gi):
        remote(block(src, n, gi, 1, NP - 1), block(dst, n, gi, 1, NP - 1), s.at[n, gi], r.at[n, gi], pdev(1)).wait_send()

    def xcopy(n, gi, way):
        src, dst = (0, 3) if way == 0 else (1, 2)
        return remote(rows.at[n, src, gi], rows.at[n, dst, gi], xs.at[n, gi, way], xr.at[n, gi, way],
                      xdev(1 if way == 0 else -1))

    def build(gi):
        row = lax.broadcasted_iota(jnp.int32, (ROWS, 64), 0)
        d = jnp.zeros((ROWS, 64), jnp.int32)
        for j in range(1, NP):
            d = d + jnp.where(row >= j * GR, 1, 0)
        e_of = z * NP + lax.rem(p + d, NP)
        pick = jnp.where(lax.broadcasted_iota(jnp.int32, (ROWS, 64), 1) == e_of, 1.0, 0.0).astype(BF16)
        row = lax.broadcasted_iota(jnp.int32, (ROWS, 128), 0)
        d = jnp.zeros((ROWS, 128), jnp.int32)
        for j in range(1, NP):
            d = d + jnp.where(row >= j * GR, 1, 0)
        within = (row - d * GR).astype(F32)
        for i in range(4):
            m = meta[4 * gi + i]
            s = dot(pick, m[0:64])
            gx = dot(pick, m[64:128])
            hit = s + float(CAP * i) == within
            pm[gi, :, pl.ds(i * 128, 128)] = jnp.where(hit, 1.0, 0.0).astype(BF16)
            wt[gi, pl.ds(i * 128, 128), :] = jnp.where(hit, gx, 0.0).T.astype(BF16)

    def gather(n, gi):
        for ab in range(2):
            yout[n, ab, gi] = dot(pm[gi], zbuf[n, ab, 4 * gi:4 * gi + 4].reshape(4 * T, w)).astype(BF16)

    def up_to(n, gi, first):
        def one(r, _):
            wk = wgu[pl.ds(cols(r, n), w), :]
            acc[gi] = acc[gi] + dot(rows[n, r, gi], wk)
            return 0
        lax.fori_loop(first, first + 2, one, 0)

    def there(t, _):
        n0, n1, n2, n3 = t, t - 1, t - 2, t - 3
        def on(n):
            return pl.when(jnp.logical_and(n >= 0, n < C))

        @on(n0)
        def _():
            for ab in range(2):
                zbuf[n0, ab, 0] = tok[:, pl.ds(cols(ab, n0), w)]
            zstart(n0, 1)

        @on(n1)
        def _():
            zstart(n1, 3)

        @on(n0)
        def _():
            zwait(n0, 1)
            zstart(n0, 2)

        @on(n1)
        def _():
            zwait(n1, 3)
            zstart(n1, 4)

        @on(n0)
        def _():
            zwait(n0, 2)

            @pl.when(n0 == 0)
            def _():
                build(0)
            gather(n0, 0)
            ystart(yout, rows, ys, yr, yl, n0, 0, 1)

        @on(n1)
        def _():
            zwait(n1, 4)

            @pl.when(n1 == 0)
            def _():
                build(1)
            gather(n1, 1)
            ystart(yout, rows, ys, yr, yl, n1, 1, 1)
            ywait(yout, rows, ys, yr, yl, n1, 0)
            for way in range(2):
                xcopy(n1, 0, way).start()

            @pl.when(n1 == 0)
            def _():
                w_copies[0].wait()
                w_copies[1].wait()
            up_to(n1, 0, 0)

        @on(n2)
        def _():
            ywait(yout, rows, ys, yr, yl, n2, 1)
            for way in range(2):
                xcopy(n2, 1, way).start()
            up_to(n2, 1, 0)
            for way in range(2):
                xcopy(n2, 0, way).wait_recv()
            up_to(n2, 0, 2)

        @on(n3)
        def _():
            for way in range(2):
                xcopy(n3, 1, way).wait_recv()
            up_to(n3, 1, 2)
        return 0

    lax.fori_loop(0, C + 3, there, 0)

    def left(n, _):
        for way in range(2):
            for h in range(1, 5):
                zcopy(n, way, h).wait_send()
        for gi in range(2):
            ysent(yout, rows, ys, yr, n, gi)
            for way in range(2):
                xcopy(n, gi, way).wait_send()
        return 0

    lax.fori_loop(0, C, left, 0)
    for h in range(1, 5):
        for way in range(2 if h < 4 else 1):
            mcopy(way, h).wait_send()

    def activate(i, _):
        for gi in range(2):
            at = pl.ds(pl.multiple_of(i * 64, 64), 64)
            gate = acc[gi, at, 0:FF]
            up = acc[gi, at, FF:2 * FF]
            hid[gi, at, :] = (gate / (1.0 + jnp.exp(-gate)) * up).astype(BF16)
        return 0

    lax.fori_loop(0, ROWS // 64, activate, 0)
    w_copies[2].wait()

    def x2copy(n, gi, way):
        return remote(yout.at[n, way, gi], pxin.at[n, 1 - way, gi], xs2.at[n, gi, way], xr2.at[n, gi, way],
                      xdev(1 if way == 0 else -1))

    def down(n, gi, r):
        return dot(hid[gi], wd[:, pl.ds(cols(r, n), w)])

    def z2copy(n, way, h):
        slot = (3 + h) if way == 0 else (5 - h)
        part = pl.ds(0, 2) if h > 1 else pl.ds(way, 1)
        return remote(zbuf.at[n, part, POS[slot]], zrec.at[n, way, h - 1, part],
                      zs2.at[n, way, h - 1], zr2.at[n, way, h - 1], zdev(1 if way == 0 else -1))

    def z2start(n, h):
        for way in range(2):
            z2copy(n, way, h).start()

    def z2add(n, h):
        for way in range(2):
            z2copy(n, way, h).wait_recv()
            slot = POS[(4 + h) if way == 0 else (4 - h)]
            for ab in range(2) if h > 1 else (way,):
                zbuf[n, ab, slot] = (zbuf[n, ab, slot].astype(F32) + zrec[n, way, h - 1, ab].astype(F32)).astype(BF16)

    def combine(n, gi):
        for ab in range(2):
            s = dot(wt[gi], yret[n, ab, gi])
            zbuf[n, ab, 4 * gi:4 * gi + 4] = s.astype(BF16).reshape(4, T, w)

    def fcopy(n):
        return remote(fin_s.at[n], fin_r.at[n], fs.at[n], fr.at[n], xdev(1))

    def back(t, _):
        n0, n1, n2, n3, n4, n5 = (t - i for i in range(6))
        def on(n):
            return pl.when(jnp.logical_and(n >= 0, n < C))

        @on(n0)
        def _():
            for gi in (1, 0):
                for way in range(2):
                    yout[n0, way, gi] = down(n0, gi, 2 + way).astype(BF16)
                    x2copy(n0, gi, way).start()

        @on(n1)
        def _():
            for gi in (1, 0):
                for ab in range(2):
                    x2copy(n1, gi, 1 - ab).wait_recv()
                    rows[n1, ab, gi] = (down(n1, gi, ab) + pxin[n1, ab, gi].astype(F32)).astype(BF16)
                ystart(rows, yret, ys2, yr2, yl2, n1, gi, -1)

        @on(n2)
        def _():
            ywait(rows, yret, ys2, yr2, yl2, n2, 1)
            combine(n2, 1)
            z2start(n2, 1)

        @on(n3)
        def _():
            z2add(n3, 2)
            z2start(n3, 3)

        @on(n2)
        def _():
            ywait(rows, yret, ys2, yr2, yl2, n2, 0)
            combine(n2, 0)
            z2add(n2, 1)
            z2start(n2, 2)

        @on(n3)
        def _():
            z2add(n3, 3)
            z2start(n3, 4)

        @on(n4)
        def _():
            tot = []
            for way in range(2):
                z2copy(n4, way, 4).wait_recv()
            for ab in range(2):
                tot.append(zbuf[n4, ab, 0].astype(F32) + zrec[n4, 0, 3, ab].astype(F32) + zrec[n4, 1, 3, ab].astype(F32))
            fin_a[n4] = tot[0]
            fin_s[n4] = tot[1].astype(BF16)
            fcopy(n4).start()

        @on(n5)
        def _():
            fcopy(n5).wait_recv()
            out[:, pl.ds(pl.multiple_of(n5 * w, w), w)] = (fin_a[n5] + fin_r[n5].astype(F32)).astype(BF16)
        return 0

    lax.fori_loop(0, C + 5, back, 0)

    def left_back(n, _):
        for way in range(2):
            for h in range(1, 5):
                z2copy(n, way, h).wait_send()
        for gi in range(2):
            ysent(rows, yret, ys2, yr2, n, gi)
            for way in range(2):
                x2copy(n, gi, way).wait_send()
        fcopy(n).wait_send()
        return 0

    lax.fori_loop(0, C, left_back, 0)


def local(tokens, routing, gate_weights, w_gate, w_up, w_down):
    T, D = tokens.shape
    FF = w_gate.shape[2]
    w = D // NX // C
    dma = pltpu.SemaphoreType.DMA
    vm = pl.BlockSpec(memory_space=pltpu.VMEM)
    anyw = pl.BlockSpec(memory_space=pl.ANY)
    return pl.pallas_call(
        kernel,
        out_shape=jax.ShapeDtypeStruct((T, D // NX), BF16),
        in_specs=[vm, vm, vm, anyw, anyw, anyw],
        out_specs=vm,
        scratch_shapes=[
            pltpu.VMEM((C, 2, NZ, T, w), BF16),
            pltpu.VMEM((NZ, 128, 128), BF16),
            pltpu.VMEM((2, ROWS, 4 * T), BF16),
            pltpu.VMEM((2, 4 * T, ROWS), BF16),
            pltpu.VMEM((C, 2, 2, ROWS, w), BF16),
            pltpu.VMEM((C, 4, 2, ROWS, w), BF16),
            pltpu.VMEM((2, ROWS, 2 * FF), F32),
            pltpu.VMEM((D, 2 * FF), BF16),
            pltpu.VMEM((FF, D), BF16),
            pltpu.VMEM((2, ROWS, FF), BF16),
            pltpu.VMEM((C, 2, 2, ROWS, w), BF16),
            pltpu.VMEM((C, 2, 2, ROWS, w), BF16),
            pltpu.VMEM((C, 2, 4, 2, T, w), BF16),
            pltpu.VMEM((C, T, w), F32),
            pltpu.VMEM((C, T, w), BF16),
            pltpu.VMEM((C, T, w), BF16),
            dma((3,)),
            dma((C, 2, 4)), dma((C, 2, 4)),
            dma((2, 4)), dma((2, 4)),
            dma((C, 2)), dma((C, 2)), dma((C, 2)),
            dma((C, 2, 2)), dma((C, 2, 2)),
            dma((C, 2, 4)), dma((C, 2, 4)),
            dma((C, 2)), dma((C, 2)), dma((C, 2)),
            dma((C, 2, 2)), dma((C, 2, 2)),
            dma((C,)), dma((C,)),
        ],
        compiler_params=pltpu.CompilerParams(
            collective_id=0, has_side_effects=True, vmem_limit_bytes=60 * 1024 * 1024
        ),
        cost_estimate=pl.CostEstimate(flops=16_000_000_000, bytes_accessed=11_000_000, transcendentals=500_000),
    )(tokens, routing, gate_weights, w_gate, w_up, w_down)


def solution(mesh):
    return jax.shard_map(
        local,
        mesh=mesh,
        in_specs=(
            P("expert", None),
            P("expert", None),
            P("expert", None),
            P("expert", None, "tensor"),
            P("expert", None, "tensor"),
            P("expert", "tensor", None),
        ),
        out_specs=P("expert", "tensor"),
        check_vma=False,
    )
```

time: 655 us -> 204 us (0.31)
  blocking collectives: 288 us -> 0 us
  Pallas kernels: 0 us -> 195 us
  waiting for transfers between devices: 170 us -> 0 us
  local copies, waits for them, and re-layouts: 100 us -> 4.49 us
  other arithmetic: 42.2 us -> 0 us
  matrix products: 27.5 us -> 0 us
  between operations: 13.5 us -> 0.01 us
  starting transfers between devices: 10.9 us -> 0 us
    all_to_all x1 -> x0, blocking collectives: 288 us -> none  [local(): lax.all_to_all(outgoing, 'expert', split_axis=0, concat_axis=0, tiled=True)]
    pallas_call x0 -> x1, Pallas kernels: none -> 195 us  [local(): pl.pallas_call(kernel, out_shape=jax.ShapeDtypeStruct((T, D // NX), BF16)...]
    reduce_scatter x1 -> x0, waiting for transfers between devices: 96.4 us -> none  [local(): lax.psum_scatter(partial_term.astype(jnp.bfloat16), 'tensor', scatter_dim...]
    all_to_all x1 -> x0, waiting for transfers between devices: 73.6 us -> none  [local(): lax.all_to_all(summed.reshape(experts, capacity, -1).astype(jnp.bfloat16)...]
    gather x3 -> x0, local copies, waits for them, and re-layouts: 43 us -> none  [the longest x2 34 us: local(): tokens[owners] * filled[:, None]]
    another operation x3 -> x0, other arithmetic: 32 us -> none
    dot_general x2 -> x0, matrix products: 27.5 us -> none  [the longest x1 17.3 us: local(): jnp.dot(hidden, w_down[0], preferred_element_type=jnp.float32)]
    reshape x2 -> x0, local copies, waits for them, and re-layouts: 19.5 us -> none  [the longest x1 14 us: local(): rows_in = arrived.reshape(-1, features)]
  transfers between devices with their start and end apart: 2 -> 0, of which waited for: 2 -> 0; matrix products, arithmetic and copies ran while one was open for 0% -> 0% of each run, Pallas kernels for 0% -> 0%
where the time goes in v1:
time: 204 us; the launch traced here: 200 us
  Pallas kernels  195 us (96%)
  local copies, waits for them, and re-layouts  4.49 us (2%)
    pallas_call x1, Pallas kernels, local(): pl.pallas_call(kernel, out_shape=jax.ShapeDtypeStruct((T, D // NX), BF16)...  195 us
    unnamed x3, local copies, waits for them, and re-layouts  4.49 us

profile of v1, /device:TPU:8, one launch (start us, length us, event | category | flops | bytes accessed | tf_op | source)
XLA Modules:
  0.0 200.0 jit_solution(3490226492433781018)
XLA Ops:
  0.0 1.4 copy.7.rt
  1.4 1.4 copy.8.gw
  2.8 195.5 %shard_map.64 = bf16[128,1024]{1,0:T(8,128)(2,1)} custom-call(bf16[128,4096]{1,0:T(8,128)(2,1)} %tok.1, s32[128,8]{1,0:T(8,128)} %copy.7.rt, f32[128,8]{1,0:T(8,128)} %copy.8.gw, bf16[1,4096,384]{2,1,0:T(8,128)(2,1)} %wg_h.1, bf16[1,4096,384]{2,1,0:T(8,128)(2,1)} %wu_h.1, bf16[1,384,4096]{2,1,0:T(8,128)(2,1)} %wd_h.1), custom_call_target="tpu_custom_call" | custom-call | flops 16000000000 | bytes 11000000 | tf_op jit(solution)/shard_map/pallas_call | solution.py:381
  198.3 1.7 copy.10

commit v2 on v0

v2 whole, which is shorter than its diff:
```python
import jax
import jax.numpy as jnp
from jax import lax
from jax.experimental import pallas as pl
from jax.experimental.pallas import tpu as pltpu
from jax.sharding import PartitionSpec as P

MESH = pl.DeviceIdType.MESH
F32, BF16 = jnp.float32, jnp.bfloat16

NZ = 8
NP = 8
NX = 4
HEAD = 16
TAIL = 4
C = 4
U = 5
B = 2 * HEAD
ROWS = NP * B
LY, LX = 2, 4
POS = {0: 0, 1: 1, 7: 2, 2: 3, 6: 4, 3: 5, 5: 6, 4: 7}


def dot(a, b):
    return jnp.dot(a, b, preferred_element_type=F32)


def kernel(rt, gw, tok, wg_h, wu_h, wd_h, out, zbuf, meta, pm, pt, wt, wtt, yout, rows, acc, wgu, wd, hid,
           pxin, yret, zrec, fin_a, fin_s, fin_r,
           w_sem, zs, zr, ms, mr, ys, yr, yl, xs, xr, zs2, zr2, ys2, yr2, yl2, xs2, xr2, fs, fr):
    T, D = tok.shape
    Q = D // NX
    w = Q // C
    FF = hid.shape[2]
    ex = lax.axis_index("expert")
    x = lax.axis_index("tensor")
    z, p = ex // NP, ex % NP

    def zdev(step):
        return (lax.rem(z + step + NZ, NZ) * NP + p, x)

    def pdev(d):
        return (z * NP + lax.rem(p + d + NP, NP), x)

    def xdev(step):
        return (ex, lax.rem(x + step + NX, NX))

    def remote(src, dst, s, r, dev):
        return pltpu.make_async_remote_copy(src_ref=src, dst_ref=dst, send_sem=s, recv_sem=r,
                                            device_id=dev, device_id_type=MESH)

    barrier = pltpu.get_barrier_semaphore()
    peers = [zdev(1), zdev(-1), xdev(1), xdev(-1)] + [pdev(d) for d in range(1, NP)]
    for dev in peers:
        pl.semaphore_signal(barrier, inc=1, device_id=dev, device_id_type=MESH)

    w_copies = [
        pltpu.make_async_copy(wg_h.at[0], wgu.at[:, pl.ds(0, FF)], w_sem.at[0]),
        pltpu.make_async_copy(wu_h.at[0], wgu.at[:, pl.ds(FF, FF)], w_sem.at[1]),
        pltpu.make_async_copy(wd_h.at[0], wd, w_sem.at[2]),
    ]
    for c in w_copies:
        c.start()

    def cols(r, n):
        return pl.multiple_of(lax.rem(x + r, NX) * Q + n * w, w)

    NE = NZ * NP
    expert = lax.broadcasted_iota(jnp.int32, (NE, T), 0)
    a = jnp.zeros((NE, T), F32)
    g = jnp.zeros((NE, T), F32)
    for k in range(rt.shape[0]):
        hit = rt[k:k + 1, :] == expert
        a = a + jnp.where(hit, 1.0, 0.0)
        g = g + jnp.where(hit, gw[k:k + 1, :], 0.0)
    earlier = jnp.where(lax.broadcasted_iota(jnp.int32, (T, T), 0) < lax.broadcasted_iota(jnp.int32, (T, T), 1),
                        1.0, 0.0).astype(BF16)
    rank = jnp.where(a > 0.0, dot(a.astype(BF16), earlier), -64.0)
    meta[0, 0:NE, :] = rank.astype(BF16)
    meta[0, NE:2 * NE, :] = g.astype(BF16)

    def own(n, _):
        for ab in range(2):
            zbuf[n, ab, 0] = tok[:, pl.ds(cols(ab, n), w)]
        return 0

    lax.fori_loop(0, C, own, 0)
    acc[...] = jnp.zeros_like(acc)
    pl.semaphore_wait(barrier, len(peers))

    def zcopy(n, way, h):
        src, dst = (h - 1, h) if way == 0 else ((NZ - h + 1) % NZ, NZ - h)
        part = pl.ds(0, 2) if h < 4 else pl.ds(way, 1)
        return remote(zbuf.at[n, part, POS[src]], zbuf.at[n, part, POS[dst]],
                      zs.at[n, way, h - 1], zr.at[n, way, h - 1], zdev(1 if way == 0 else -1))

    def mcopy(way, h):
        src, dst = (h - 1, h) if way == 0 else ((NZ - h + 1) % NZ, NZ - h)
        return remote(meta.at[POS[src]], meta.at[POS[dst]],
                      ms.at[way, h - 1], mr.at[way, h - 1], zdev(1 if way == 0 else -1))

    def zstart(n, h):
        @pl.when(n == 0)
        def _():
            for way in range(2 if h < 4 else 1):
                mcopy(way, h).start()
        for way in range(2):
            zcopy(n, way, h).start()

    def zwait(n, h):
        @pl.when(n == 0)
        def _():
            for way in range(2 if h < 4 else 1):
                mcopy(way, h).wait_recv()
        for way in range(2):
            zcopy(n, way, h).wait_recv()

    def block(ref, n, u, d, count=1):
        return ref.at[n, pl.ds(0, 2), u, pl.ds(pl.multiple_of(d * B, 16), count * B)]

    def ystart(src, dst, s, r, loc, n, u, sign):
        def one(d, _):
            remote(block(src, n, u, d), block(dst, n, u, d), s.at[n, u], r.at[n, u], pdev(sign * d)).start()
            return 0
        lax.fori_loop(1, NP, one, 0)
        pltpu.make_async_copy(block(src, n, u, 0), block(dst, n, u, 0), loc.at[n, u]).start()

    def ywait(src, dst, s, r, loc, n, u):
        remote(block(src, n, u, 1, NP - 1), block(dst, n, u, 1, NP - 1), s.at[n, u], r.at[n, u], pdev(1)).wait_recv()
        pltpu.make_async_copy(block(src, n, u, 0), block(dst, n, u, 0), loc.at[n, u]).wait()

    def ysent(src, dst, s, r, n, u):
        remote(block(src, n, u, 1, NP - 1), block(dst, n, u, 1, NP - 1), s.at[n, u], r.at[n, u], pdev(1)).wait_send()

    def xcopy(n, u, way):
        src, dst = (0, 3) if way == 0 else (1, 2)
        return remote(rows.at[n, src, u], rows.at[n, dst, u], xs.at[n, u, way], xr.at[n, u, way],
                      xdev(1 if way == 0 else -1))

    def build(pair):
        row = lax.broadcasted_iota(jnp.int32, (ROWS, NE), 0)
        e_of = z * NP + lax.rem(p + lax.shift_right_logical(row, 5), NP)
        pick = jnp.where(lax.broadcasted_iota(jnp.int32, (ROWS, NE), 1) == e_of, 1.0, 0.0).astype(BF16)
        row = lax.broadcasted_iota(jnp.int32, (ROWS, T), 0)
        within = (row & (B - 1)).astype(F32)
        for b in range(2):
            pos = 2 * pair + b
            m = meta[pos]
            s = dot(pick, m[0:NE])
            gx = dot(pick, m[NE:2 * NE])
            head = jnp.logical_and(s + float(HEAD * b) == within, s < float(HEAD))
            tail = jnp.logical_and(s + float(TAIL * pos - HEAD) == within, s >= float(HEAD))
            pm[pair, :, pl.ds(b * T, T)] = jnp.where(head, 1.0, 0.0).astype(BF16)
            pt[:, pl.ds(pos * T, T)] = jnp.where(tail, 1.0, 0.0).astype(BF16)
            wt[pair, pl.ds(b * T, T), :] = jnp.where(head, gx, 0.0).T.astype(BF16)
            wtt[pl.ds(pos * T, T), :] = jnp.where(tail, gx, 0.0).T.astype(BF16)

    def gather(n, u):
        @pl.when(u < U - 1)
        def _():
            for ab in range(2):
                yout[n, ab, u] = dot(pm[u], zbuf[n, ab, pl.ds(2 * u, 2)].reshape(2 * T, w)).astype(BF16)

        @pl.when(u == U - 1)
        def _():
            for ab in range(2):
                yout[n, ab, u] = dot(pt[...], zbuf[n, ab].reshape(NZ * T, w)).astype(BF16)

    def up_to(n, u, first):
        def one(r, _):
            acc[u] = acc[u] + dot(rows[n, r, u], wgu[pl.ds(cols(r, n), w), :])
            return 0
        lax.fori_loop(first, first + 2, one, 0)

    def activate(u):
        def one(i, _):
            at = pl.ds(pl.multiple_of(i * 64, 64), 64)
            gate = acc[u, at, 0:FF]
            hid[u, at, :] = (gate / (1.0 + jnp.exp(-gate)) * acc[u, at, FF:2 * FF]).astype(BF16)
            return 0
        lax.fori_loop(0, ROWS // 64, one, 0)

    def on(i):
        return pl.when(jnp.logical_and(i >= 0, i < U * C))

    for n in range(2):
        zstart(n, 1)

    def there(i, _):
        u, n = lax.div(i, C), lax.rem(i, C)
        j, k = i - LY, i - LX
        ju, jn = lax.div(j, C), lax.rem(j, C)
        ku, kn = lax.div(k, C), lax.rem(k, C)

        @on(i)
        def _():
            for pair in range(4):
                @pl.when(u == pair)
                def _():
                    zwait(n, pair + 1)
                    if pair < 3:
                        zstart(n, pair + 2)
                    if pair == 0:
                        @pl.when(n < C - 2)
                        def _():
                            zstart(n + 2, 1)

                    @pl.when(n == 0)
                    def _():
                        build(pair)
            gather(n, u)
            ystart(yout, rows, ys, yr, yl, n, u, 1)

        @pl.when(i == LY)
        def _():
            w_copies[0].wait()
            w_copies[1].wait()

        @on(j)
        def _():
            ywait(yout, rows, ys, yr, yl, jn, ju)
            for way in range(2):
                xcopy(jn, ju, way).start()
            up_to(jn, ju, 0)

        @on(k)
        def _():
            for way in range(2):
                xcopy(kn, ku, way).wait_recv()
            up_to(kn, ku, 2)

            @pl.when(kn == C - 1)
            def _():
                activate(ku)
        return 0

    lax.fori_loop(0, U * C + LX, there, 0)

    def left(n, _):
        for way in range(2):
            for h in range(1, 5):
                zcopy(n, way, h).wait_send()

        def unit(u, _):
            ysent(yout, rows, ys, yr, n, u)
            for way in range(2):
                xcopy(n, u, way).wait_send()
            return 0
        lax.fori_loop(0, U, unit, 0)
        return 0

    lax.fori_loop(0, C, left, 0)
    for h in range(1, 5):
        for way in range(2 if h < 4 else 1):
            mcopy(way, h).wait_send()
    w_copies[2].wait()

    def x2copy(n, u, way):
        return remote(yout.at[n, way, u], pxin.at[n, 1 - way, u], xs2.at[n, u, way], xr2.at[n, u, way],
                      xdev(1 if way == 0 else -1))

    def down(n, u, r):
        return dot(hid[u], wd[:, pl.ds(cols(r, n), w)])

    def z2copy(n, way, h):
        slot = (3 + h) if way == 0 else (5 - h)
        part = pl.ds(0, 2) if h > 1 else pl.ds(way, 1)
        return remote(zbuf.at[n, part, POS[slot]], zrec.at[n, way, h - 1, part],
                      zs2.at[n, way, h - 1], zr2.at[n, way, h - 1], zdev(1 if way == 0 else -1))

    def z2start(n, h):
        for way in range(2):
            z2copy(n, way, h).start()

    def z2add(n, h):
        for way in range(2):
            z2copy(n, way, h).wait_recv()
            slot = POS[(4 + h) if way == 0 else (4 - h)]
            for ab in range(2) if h > 1 else (way,):
                zbuf[n, ab, slot] = (zbuf[n, ab, slot].astype(F32) + zrec[n, way, h - 1, ab].astype(F32)).astype(BF16)

    def combine(n, u):
        @pl.when(u < U - 1)
        def _():
            at = pl.ds(2 * u, 2)
            for ab in range(2):
                s = dot(wt[u], yret[n, ab, u]).reshape(2, T, w)
                zbuf[n, ab, at] = (zbuf[n, ab, at].astype(F32) + s).astype(BF16)

        @pl.when(u == U - 1)
        def _():
            for ab in range(2):
                zbuf[n, ab] = dot(wtt[...], yret[n, ab, u]).astype(BF16).reshape(NZ, T, w)

    def fcopy(n):
        return remote(fin_s.at[n], fin_r.at[n], fs.at[n], fr.at[n], xdev(1))

    def back(i, _):
        j, k = i - LY, i - LX
        u, n = U - 1 - lax.div(i, C), lax.rem(i, C)
        ju, jn = U - 1 - lax.div(j, C), lax.rem(j, C)
        ku, kn = U - 1 - lax.div(k, C), lax.rem(k, C)

        @on(i)
        def _():
            for way in range(2):
                yout[n, way, u] = down(n, u, 2 + way).astype(BF16)
                x2copy(n, u, way).start()

        @on(j)
        def _():
            for ab in range(2):
                x2copy(jn, ju, 1 - ab).wait_recv()
                rows[jn, ab, ju] = (down(jn, ju, ab) + pxin[jn, ab, ju].astype(F32)).astype(BF16)
            ystart(rows, yret, ys2, yr2, yl2, jn, ju, -1)

        @on(k)
        def _():
            ywait(rows, yret, ys2, yr2, yl2, kn, ku)
            combine(kn, ku)
            for h in range(1, 5):
                @pl.when(ku == 4 - h)
                def _():
                    if h > 1:
                        z2add(kn, h - 1)
                    z2start(kn, h)
        return 0

    lax.fori_loop(0, U * C + LX, back, 0)

    def finish(n, _):
        tot = []
        for way in range(2):
            z2copy(n, way, 4).wait_recv()
        for ab in range(2):
            tot.append(zbuf[n, ab, 0].astype(F32) + zrec[n, 0, 3, ab].astype(F32) + zrec[n, 1, 3, ab].astype(F32))
        fin_s[n] = tot[1].astype(BF16)
        fcopy(n).start()
        fin_a[n] = tot[0]
        return 0

    lax.fori_loop(0, C, finish, 0)

    def write(n, _):
        fcopy(n).wait_recv()
        out[:, pl.ds(pl.multiple_of(n * w, w), w)] = (fin_a[n] + fin_r[n].astype(F32)).astype(BF16)
        return 0

    lax.fori_loop(0, C, write, 0)

    def left_back(n, _):
        for way in range(2):
            for h in range(1, 5):
                z2copy(n, way, h).wait_send()

        def unit(u, _):
            ysent(rows, yret, ys2, yr2, n, u)
            for way in range(2):
                x2copy(n, u, way).wait_send()
            return 0
        lax.fori_loop(0, U, unit, 0)
        fcopy(n).wait_send()
        return 0

    lax.fori_loop(0, C, left_back, 0)


def local(tokens, routing, gate_weights, w_gate, w_up, w_down):
    T, D = tokens.shape
    FF = w_gate.shape[2]
    w = D // NX // C
    dma = pltpu.SemaphoreType.DMA
    vm = pl.BlockSpec(memory_space=pltpu.VMEM)
    anyw = pl.BlockSpec(memory_space=pl.ANY)
    return pl.pallas_call(
        kernel,
        out_shape=jax.ShapeDtypeStruct((T, D // NX), BF16),
        in_specs=[vm, vm, vm, anyw, anyw, anyw],
        out_specs=vm,
        scratch_shapes=[
            pltpu.VMEM((C, 2, NZ, T, w), BF16),
            pltpu.VMEM((NZ, 128, T), BF16),
            pltpu.VMEM((U - 1, ROWS, 2 * T), BF16),
            pltpu.VMEM((ROWS, NZ * T), BF16),
            pltpu.VMEM((U - 1, 2 * T, ROWS), BF16),
            pltpu.VMEM((NZ * T, ROWS), BF16),
            pltpu.VMEM((C, 2, U, ROWS, w), BF16),
            pltpu.VMEM((C, 4, U, ROWS, w), BF16),
            pltpu.VMEM((U, ROWS, 2 * FF), F32),
            pltpu.VMEM((D, 2 * FF), BF16),
            pltpu.VMEM((FF, D), BF16),
            pltpu.VMEM((U, ROWS, FF), BF16),
            pltpu.VMEM((C, 2, U, ROWS, w), BF16),
            pltpu.VMEM((C, 2, U, ROWS, w), BF16),
            pltpu.VMEM((C, 2, 4, 2, T, w), BF16),
            pltpu.VMEM((C, T, w), F32),
            pltpu.VMEM((C, T, w), BF16),
            pltpu.VMEM((C, T, w), BF16),
            dma((3,)),
            dma((C, 2, 4)), dma((C, 2, 4)),
            dma((2, 4)), dma((2, 4)),
            dma((C, U)), dma((C, U)), dma((C, U)),
            dma((C, U, 2)), dma((C, U, 2)),
            dma((C, 2, 4)), dma((C, 2, 4)),
            dma((C, U)), dma((C, U)), dma((C, U)),
            dma((C, U, 2)), dma((C, U, 2)),
            dma((C,)), dma((C,)),
        ],
        compiler_params=pltpu.CompilerParams(
            collective_id=0, has_side_effects=True, vmem_limit_bytes=60 * 1024 * 1024
        ),
        cost_estimate=pl.CostEstimate(flops=16_000_000_000, bytes_accessed=11_000_000, transcendentals=500_000),
    )(routing.T, gate_weights.T, tokens, w_gate, w_up, w_down)


def solution(mesh):
    return jax.shard_map(
        local,
        mesh=mesh,
        in_specs=(
            P("expert", None),
            P("expert", None),
            P("expert", None),
            P("expert", None, "tensor"),
            P("expert", None, "tensor"),
            P("expert", "tensor", None),
        ),
        out_specs=P("expert", "tensor"),
        check_vma=False,
    )
```

time: 655 us -> 170 us (0.26)
  blocking collectives: 288 us -> 0 us
  waiting for transfers between devices: 170 us -> 0 us
  Pallas kernels: 0 us -> 167 us
  local copies, waits for them, and re-layouts: 100 us -> 1.67 us
  other arithmetic: 42.2 us -> 0 us
  matrix products: 27.5 us -> 0 us
  between operations: 13.5 us -> 0.01 us
  starting transfers between devices: 10.9 us -> 0 us
    all_to_all x1 -> x0, blocking collectives: 288 us -> none  [local(): lax.all_to_all(outgoing, 'expert', split_axis=0, concat_axis=0, tiled=True)]
    pallas_call x0 -> x1, Pallas kernels: none -> 167 us  [local(): pl.pallas_call(kernel, out_shape=jax.ShapeDtypeStruct((T, D // NX), BF16)...]
    reduce_scatter x1 -> x0, waiting for transfers between devices: 96.4 us -> none  [local(): lax.psum_scatter(partial_term.astype(jnp.bfloat16), 'tensor', scatter_dim...]
    all_to_all x1 -> x0, waiting for transfers between devices: 73.6 us -> none  [local(): lax.all_to_all(summed.reshape(experts, capacity, -1).astype(jnp.bfloat16)...]
    gather x3 -> x0, local copies, waits for them, and re-layouts: 43 us -> none  [the longest x2 34 us: local(): tokens[owners] * filled[:, None]]
    another operation x3 -> x0, other arithmetic: 32 us -> none
    dot_general x2 -> x0, matrix products: 27.5 us -> none  [the longest x1 17.3 us: local(): jnp.dot(hidden, w_down[0], preferred_element_type=jnp.float32)]
    reshape x2 -> x0, local copies, waits for them, and re-layouts: 19.5 us -> none  [the longest x1 14 us: local(): rows_in = arrived.reshape(-1, features)]
  transfers between devices with their start and end apart: 2 -> 0, of which waited for: 2 -> 0; matrix products, arithmetic and copies ran while one was open for 0% -> 0% of each run, Pallas kernels for 0% -> 0%
where the time goes in v2:
time: 170 us; the launch traced here: 169 us
  Pallas kernels  167 us (98%)
    pallas_call x1, Pallas kernels, local(): pl.pallas_call(kernel, out_shape=jax.ShapeDtypeStruct((T, D // NX), BF16)...  167 us

profile of v2, /device:TPU:8, one launch (start us, length us, event | category | flops | bytes accessed | tf_op | source)
XLA Modules:
  0.0 168.7 jit_solution(5657994374877673288)
XLA Ops:
  0.0 167.1 %shard_map.64 = bf16[128,1024]{1,0:T(8,128)(2,1)} custom-call(s32[8,128]{1,0:T(8,128)} %bitcast.2, f32[8,128]{1,0:T(8,128)} %bitcast.3, bf16[128,4096]{1,0:T(8,128)(2,1)} %tok.1, bf16[1,4096,384]{2,1,0:T(8,128)(2,1)} %wg_h.1, bf16[1,4096,384]{2,1,0:T(8,128)(2,1)} %wu_h.1, bf16[1,384,4096]{2,1,0:T(8,128)(2,1)} %wd_h.1), custom_call_target="tpu_custom_call" | custom-call | flops 16000000000 | bytes 11000000 | tf_op jit(solution)/shard_map/pallas_call | solution.py:375
  167.1 1.7 copy.8

commit v3 on v2

--- a/solution.py
+++ b/solution.py
@@ -18,6 +18,8 @@
 B = 2 * HEAD
 ROWS = NP * B
 LY, LX = 2, 4
+KX, KY = 2, 4
+R0 = (U - 1) * C + LX - 1
 POS = {0: 0, 1: 1, 7: 2, 2: 3, 6: 4, 3: 5, 5: 6, 4: 7}
 
 
@@ -183,10 +185,53 @@
     def on(i):
         return pl.when(jnp.logical_and(i >= 0, i < U * C))
 
-    for n in range(2):
+    def x2copy(n, u, way):
+        return remote(yout.at[n, way, u], pxin.at[n, 1 - way, u], xs2.at[n, u, way], xr2.at[n, u, way],
+                      xdev(1 if way == 0 else -1))
+
+    def down(n, u, r):
+        return dot(hid[u], wd[:, pl.ds(cols(r, n), w)])
+
+    def z2copy(n, way, h):
+        slot = (3 + h) if way == 0 else (5 - h)
+        part = pl.ds(0, 2) if h > 1 else pl.ds(way, 1)
+        return remote(zbuf.at[n, part, POS[slot]], zrec.at[n, way, h - 1, part],
+                      zs2.at[n, way, h - 1], zr2.at[n, way, h - 1], zdev(1 if way == 0 else -1))
+
+    def z2start(n, h):
+        for way in range(2):
+            z2copy(n, way, h).start()
+
+    def z2add(n, h):
+        for way in range(2):
+            z2copy(n, way, h).wait_recv()
+            slot = POS[(4 + h) if way == 0 else (4 - h)]
+            for ab in range(2) if h > 1 else (way,):
+                zbuf[n, ab, slot] = (zbuf[n, ab, slot].astype(F32) + zrec[n, way, h - 1, ab].astype(F32)).astype(BF16)
+
+    def combine(n, u):
+        @pl.when(u < U - 1)
+        def _():
+            at = pl.ds(2 * u, 2)
+            for ab in range(2):
+                c = dot(wt[u], yret[n, ab, u]).reshape(2, T, w)
+                before = jnp.where(u == 3, 0.0, zbuf[n, ab, at].astype(F32))
+                zbuf[n, ab, at] = (before + c).astype(BF16)
+
+        @pl.when(u == U - 1)
+        def _():
+            for ab in range(2):
+                c = dot(wtt[...], yret[n, ab, u]).reshape(NZ, T, w)
+                zbuf[n, ab, 0:6] = c[0:6].astype(BF16)
+                zbuf[n, ab, 6:8] = (zbuf[n, ab, 6:8].astype(F32) + c[6:8]).astype(BF16)
+
+    def fcopy(n):
+        return remote(fin_s.at[n], fin_r.at[n], fs.at[n], fr.at[n], xdev(1))
+
+    for n in range(4):
         zstart(n, 1)
 
-    def there(i, _):
+    def step(i, _):
         u, n = lax.div(i, C), lax.rem(i, C)
         j, k = i - LY, i - LX
         ju, jn = lax.div(j, C), lax.rem(j, C)
@@ -200,10 +245,6 @@
                     zwait(n, pair + 1)
                     if pair < 3:
                         zstart(n, pair + 2)
-                    if pair == 0:
-                        @pl.when(n < C - 2)
-                        def _():
-                            zstart(n + 2, 1)
 
                     @pl.when(n == 0)
                     def _():
@@ -232,101 +273,57 @@
             @pl.when(kn == C - 1)
             def _():
                 activate(ku)
+
+        r = i - R0
+        rj, rk = r - KX, r - KY
+
+        def unit(q):
+            return jnp.where(q == 0, 3, jnp.where(q == 1, 4, 4 - q))
+        ru, rn = unit(lax.div(r, C)), lax.rem(r, C)
+        rju, rjn = unit(lax.div(rj, C)), lax.rem(rj, C)
+        rku, rkn = unit(lax.div(rk, C)), lax.rem(rk, C)
+
+        @pl.when(r == 0)
+        def _():
+            w_copies[2].wait()
+
+        @on(r)
+        def _():
+            ysent(yout, rows, ys, yr, rn, ru)
+            for way in range(2):
+                yout[rn, way, ru] = down(rn, ru, 2 + way).astype(BF16)
+                x2copy(rn, ru, way).start()
+
+        @on(rj)
+        def _():
+            for ab in range(2):
+                xcopy(rjn, rju, ab).wait_send()
+                x2copy(rjn, rju, 1 - ab).wait_recv()
+                rows[rjn, ab, rju] = (down(rjn, rju, ab) + pxin[rjn, ab, rju].astype(F32)).astype(BF16)
+            ystart(rows, yret, ys2, yr2, yl2, rjn, rju, -1)
+
+        @on(rk)
+        def _():
+            ywait(rows, yret, ys2, yr2, yl2, rkn, rku)
+
+            @pl.when(rku == 3)
+            def _():
+                for way in range(2):
+                    for h in range(1, 5):
+                        zcopy(rkn, way, h).wait_send()
+            combine(rkn, rku)
+            for v, h in ((4, 1), (2, 2), (1, 3), (0, 4)):
+                @pl.when(rku == v)
+                def _():
+                    if h > 1:
+                        z2add(rkn, h - 1)
+                    z2start(rkn, h)
         return 0
 
-    lax.fori_loop(0, U * C + LX, there, 0)
-
-    def left(n, _):
-        for way in range(2):
-            for h in range(1, 5):
-                zcopy(n, way, h).wait_send()
-
-        def unit(u, _):
-            ysent(yout, rows, ys, yr, n, u)
-            for way in range(2):
-                xcopy(n, u, way).wait_send()
-            return 0
-        lax.fori_loop(0, U, unit, 0)
-        return 0
-
-    lax.fori_loop(0, C, left, 0)
+    lax.fori_loop(0, R0 + U * C + KY, step, 0)
     for h in range(1, 5):
         for way in range(2 if h < 4 else 1):
             mcopy(way, h).wait_send()
-    w_copies[2].wait()
-
-    def x2copy(n, u, way):
-        return remote(yout.at[n, way, u], pxin.at[n, 1 - way, u], xs2.at[n, u, way], xr2.at[n, u, way],
-                      xdev(1 if way == 0 else -1))
-
-    def down(n, u, r):
-        return dot(hid[u], wd[:, pl.ds(cols(r, n), w)])
-
-    def z2copy(n, way, h):
-        slot = (3 + h) if way == 0 else (5 - h)
-        part = pl.ds(0, 2) if h > 1 else pl.ds(way, 1)
-        return remote(zbuf.at[n, part, POS[slot]], zrec.at[n, way, h - 1, part],
-                      zs2.at[n, way, h - 1], zr2.at[n, way, h - 1], zdev(1 if way == 0 else -1))
-
-    def z2start(n, h):
-        for way in range(2):
-            z2copy(n, way, h).start()
-
-    def z2add(n, h):
-        for way in range(2):
-            z2copy(n, way, h).wait_recv()
-            slot = POS[(4 + h) if way == 0 else (4 - h)]
-            for ab in range(2) if h > 1 else (way,):
-                zbuf[n, ab, slot] = (zbuf[n, ab, slot].astype(F32) + zrec[n, way, h - 1, ab].astype(F32)).astype(BF16)
-
-    def combine(n, u):
-        @pl.when(u < U - 1)
-        def _():
-            at = pl.ds(2 * u, 2)
-            for ab in range(2):
-                s = dot(wt[u], yret[n, ab, u]).reshape(2, T, w)
-                zbuf[n, ab, at] = (zbuf[n, ab, at].astype(F32) + s).astype(BF16)
-
-        @pl.when(u == U - 1)
-        def _():
-            for ab in range(2):
-                zbuf[n, ab] = dot(wtt[...], yret[n, ab, u]).astype(BF16).reshape(NZ, T, w)
-
-    def fcopy(n):
-        return remote(fin_s.at[n], fin_r.at[n], fs.at[n], fr.at[n], xdev(1))
-
-    def back(i, _):
-        j, k = i - LY, i - LX
-        u, n = U - 1 - lax.div(i, C), lax.rem(i, C)
-        ju, jn = U - 1 - lax.div(j, C), lax.rem(j, C)
-        ku, kn = U - 1 - lax.div(k, C), lax.rem(k, C)
-
-        @on(i)
-        def _():
-            for way in range(2):
-                yout[n, way, u] = down(n, u, 2 + way).astype(BF16)
-                x2copy(n, u, way).start()
-
-        @on(j)
-        def _():
-            for ab in range(2):
-                x2copy(jn, ju, 1 - ab).wait_recv()
-                rows[jn, ab, ju] = (down(jn, ju, ab) + pxin[jn, ab, ju].astype(F32)).astype(BF16)
-            ystart(rows, yret, ys2, yr2, yl2, jn, ju, -1)
-
-        @on(k)
-        def _():
-            ywait(rows, yret, ys2, yr2, yl2, kn, ku)
-            combine(kn, ku)
-            for h in range(1, 5):
-                @pl.when(ku == 4 - h)
-                def _():
-                    if h > 1:
-                        z2add(kn, h - 1)
-                    z2start(kn, h)
-        return 0
-
-    lax.fori_loop(0, U * C + LX, back, 0)
 
     def finish(n, _):
         tot = []

time: 170 us -> 161 us (0.947)
  Pallas kernels: 167 us -> 158 us
    pallas_call x1, Pallas kernels: 167 us -> 158 us  [local(): pl.pallas_call(kernel, out_shape=jax.ShapeDtypeStruct((T, D // NX), BF16)...]
where the time goes in v3:
time: 161 us; the launch traced here: 160 us
  Pallas kernels  158 us (98%)
  local copies, waits for them, and re-layouts  1.67 us (1%)
    pallas_call x1, Pallas kernels, local(): pl.pallas_call(kernel, out_shape=jax.ShapeDtypeStruct((T, D // NX), BF16)...  158 us

profile of v3, /device:TPU:8, one launch (start us, length us, event | category | flops | bytes accessed | tf_op | source)
XLA Modules:
  0.0 159.7 jit_solution(12132902042802569465)
XLA Ops:
  0.0 158.0 %shard_map.64 = bf16[128,1024]{1,0:T(8,128)(2,1)} custom-call(s32[8,128]{1,0:T(8,128)} %bitcast.2, f32[8,128]{1,0:T(8,128)} %bitcast.3, bf16[128,4096]{1,0:T(8,128)(2,1)} %tok.1, bf16[1,4096,384]{2,1,0:T(8,128)(2,1)} %wg_h.1, bf16[1,4096,384]{2,1,0:T(8,128)(2,1)} %wu_h.1, bf16[1,384,4096]{2,1,0:T(8,128)(2,1)} %wd_h.1), custom_call_target="tpu_custom_call" | custom-call | flops 16000000000 | bytes 11000000 | tf_op jit(solution)/shard_map/pallas_call | solution.py:372
  158.0 1.7 %copy.8 = bf16[128,1024]{1,0:T(8,128)(2,1)} copy(bf16[128,1024]{1,0:T(8,128)(2,1)} %shard_map.64) | data formatting | bytes 524288

commit v4 on v3

--- a/solution.py
+++ b/solution.py
@@ -19,17 +19,18 @@
 ROWS = NP * B
 LY, LX = 2, 4
 KX, KY = 2, 4
-R0 = (U - 1) * C + LX - 1
-POS = {0: 0, 1: 1, 7: 2, 2: 3, 6: 4, 3: 5, 5: 6, 4: 7}
+S = (U - 1) * C + C // 2
+R0 = (U - 2) * C + C // 2 - 1 + LX
+POS = {0: 0, 4: 1, 1: 2, 7: 3, 2: 4, 6: 5, 3: 6, 5: 7}
 
 
 def dot(a, b):
     return jnp.dot(a, b, preferred_element_type=F32)
 
 
-def kernel(rt, gw, tok, wg_h, wu_h, wd_h, out, zbuf, meta, pm, pt, wt, wtt, yout, rows, acc, wgu, wd, hid,
+def kernel(rt, gw, tok, wg_h, wu_h, wd_h, out, zbuf, meta, pm, pt, ph, wt, wtt, yout, rows, acc, wgu, wd, hid,
            pxin, yret, zrec, fin_a, fin_s, fin_r,
-           w_sem, zs, zr, ms, mr, ys, yr, yl, xs, xr, zs2, zr2, ys2, yr2, yl2, xs2, xr2, fs, fr):
+           w_sem, zs, zr, ms, mr, ys, yr, yl, xs, xr, zs2, zr2, ys2, yr2, yl2, ys4, yr4, yl4, xs3, xr3, xs2, xr2, fs, fr):
     T, D = tok.shape
     Q = D // NX
     w = Q // C
@@ -118,59 +119,82 @@
             zcopy(n, way, h).wait_recv()
 
     def block(ref, n, u, d, count=1):
-        return ref.at[n, pl.ds(0, 2), u, pl.ds(pl.multiple_of(d * B, 16), count * B)]
-
-    def ystart(src, dst, s, r, loc, n, u, sign):
+        return ref.at[n, pl.ds(0, 2), u, pl.ds(d, count)]
+
+    def half(ref, n, b, d, count=1):
+        return ref.at[n, pl.ds(0, 2), 0, pl.ds(d, count), pl.ds(b * HEAD, HEAD)]
+
+    def ystart(src, dst, s, r, loc, n, u, sign, b=None):
+        def part(ref, d):
+            return block(ref, n, u, d) if b is None else half(ref, n, b, d)
+
         def one(d, _):
-            remote(block(src, n, u, d), block(dst, n, u, d), s.at[n, u], r.at[n, u], pdev(sign * d)).start()
+            remote(part(src, d), part(dst, d), s, r, pdev(sign * d)).start()
             return 0
         lax.fori_loop(1, NP, one, 0)
-        pltpu.make_async_copy(block(src, n, u, 0), block(dst, n, u, 0), loc.at[n, u]).start()
-
-    def ywait(src, dst, s, r, loc, n, u):
-        remote(block(src, n, u, 1, NP - 1), block(dst, n, u, 1, NP - 1), s.at[n, u], r.at[n, u], pdev(1)).wait_recv()
-        pltpu.make_async_copy(block(src, n, u, 0), block(dst, n, u, 0), loc.at[n, u]).wait()
-
-    def ysent(src, dst, s, r, n, u):
-        remote(block(src, n, u, 1, NP - 1), block(dst, n, u, 1, NP - 1), s.at[n, u], r.at[n, u], pdev(1)).wait_send()
-
-    def xcopy(n, u, way):
+        pltpu.make_async_copy(part(src, 0), part(dst, 0), loc).start()
+
+    def yall(src, dst, s, r, n, u, b=None):
+        def part(ref):
+            return block(ref, n, u, 1, NP - 1) if b is None else half(ref, n, b, 1, NP - 1)
+        return remote(part(src), part(dst), s, r, pdev(1))
+
+    def ywait(src, dst, s, r, loc, n, u, b=None):
+        def part(ref):
+            return block(ref, n, u, 0) if b is None else half(ref, n, b, 0)
+        yall(src, dst, s, r, n, u, b).wait_recv()
+        pltpu.make_async_copy(part(src), part(dst), loc).wait()
+
+    def xcopy(n, u, way, b=None):
         src, dst = (0, 3) if way == 0 else (1, 2)
-        return remote(rows.at[n, src, u], rows.at[n, dst, u], xs.at[n, u, way], xr.at[n, u, way],
-                      xdev(1 if way == 0 else -1))
-
-    def build(pair):
-        row = lax.broadcasted_iota(jnp.int32, (ROWS, NE), 0)
-        e_of = z * NP + lax.rem(p + lax.shift_right_logical(row, 5), NP)
-        pick = jnp.where(lax.broadcasted_iota(jnp.int32, (ROWS, NE), 1) == e_of, 1.0, 0.0).astype(BF16)
-        row = lax.broadcasted_iota(jnp.int32, (ROWS, T), 0)
-        within = (row & (B - 1)).astype(F32)
-        for b in range(2):
-            pos = 2 * pair + b
-            m = meta[pos]
-            s = dot(pick, m[0:NE])
-            gx = dot(pick, m[NE:2 * NE])
-            head = jnp.logical_and(s + float(HEAD * b) == within, s < float(HEAD))
-            tail = jnp.logical_and(s + float(TAIL * pos - HEAD) == within, s >= float(HEAD))
-            pm[pair, :, pl.ds(b * T, T)] = jnp.where(head, 1.0, 0.0).astype(BF16)
-            pt[:, pl.ds(pos * T, T)] = jnp.where(tail, 1.0, 0.0).astype(BF16)
-            wt[pair, pl.ds(b * T, T), :] = jnp.where(head, gx, 0.0).T.astype(BF16)
-            wtt[pl.ds(pos * T, T), :] = jnp.where(tail, gx, 0.0).T.astype(BF16)
+
+        def part(r):
+            return rows.at[n, r, u] if b is None else rows.at[n, r, 0, :, pl.ds(b * HEAD, HEAD)]
+        s, r = (xs3.at[n, way], xr3.at[n, way]) if b == 0 else (xs.at[n, u, way], xr.at[n, u, way])
+        return remote(part(src), part(dst), s, r, xdev(1 if way == 0 else -1))
+
+    def picked(m, size, shift):
+        row = lax.broadcasted_iota(jnp.int32, (size, NE), 0)
+        e_of = z * NP + lax.rem(p + lax.shift_right_logical(row, shift), NP)
+        pick = jnp.where(lax.broadcasted_iota(jnp.int32, (size, NE), 1) == e_of, 1.0, 0.0).astype(BF16)
+        within = lax.broadcasted_iota(jnp.int32, (size, T), 0) & ((1 << shift) - 1)
+        return dot(pick, m[0:NE]), dot(pick, m[NE:2 * NE]), within.astype(F32)
+
+    def build(pos):
+        pair, b = divmod(pos, 2)
+        m = meta[pos]
+        s, gx, within = picked(m, ROWS, 5)
+        tail = jnp.logical_and(s + float(TAIL * pos - HEAD) == within, s >= float(HEAD))
+        pt[:, pl.ds(pos * T, T)] = jnp.where(tail, 1.0, 0.0).astype(BF16)
+        wtt[pl.ds(pos * T, T), :] = jnp.where(tail, gx, 0.0).T.astype(BF16)
+        head = jnp.logical_and(s + float(HEAD * b) == within, s < float(HEAD))
+        wt[pair, pl.ds(b * T, T), :] = jnp.where(head, gx, 0.0).T.astype(BF16)
+        if pair > 0:
+            pm[pair - 1, :, pl.ds(b * T, T)] = jnp.where(head, 1.0, 0.0).astype(BF16)
+        else:
+            s, gx, within = picked(m, NP * HEAD, 4)
+            ph[b] = jnp.where(s == within, 1.0, 0.0).astype(BF16)
+
+    def gather_half(n, b):
+        for ab in range(2):
+            y = dot(ph[b], zbuf[n, ab, b]).astype(BF16)
+            yout[n, ab, 0, :, b * HEAD:(b + 1) * HEAD] = y.reshape(NP, HEAD, w)
 
     def gather(n, u):
-        @pl.when(u < U - 1)
+        @pl.when(jnp.logical_and(u > 0, u < U - 1))
         def _():
             for ab in range(2):
-                yout[n, ab, u] = dot(pm[u], zbuf[n, ab, pl.ds(2 * u, 2)].reshape(2 * T, w)).astype(BF16)
+                y = dot(pm[u - 1], zbuf[n, ab, pl.ds(2 * u, 2)].reshape(2 * T, w)).astype(BF16)
+                yout[n, ab, u] = y.reshape(NP, B, w)
 
         @pl.when(u == U - 1)
         def _():
             for ab in range(2):
-                yout[n, ab, u] = dot(pt[...], zbuf[n, ab].reshape(NZ * T, w)).astype(BF16)
+                yout[n, ab, u] = dot(pt[...], zbuf[n, ab].reshape(NZ * T, w)).astype(BF16).reshape(NP, B, w)
 
     def up_to(n, u, first):
         def one(r, _):
-            acc[u] = acc[u] + dot(rows[n, r, u], wgu[pl.ds(cols(r, n), w), :])
+            acc[u] = acc[u] + dot(rows[n, r, u].reshape(ROWS, w), wgu[pl.ds(cols(r, n), w), :])
             return 0
         lax.fori_loop(first, first + 2, one, 0)
 
@@ -214,71 +238,130 @@
         def _():
             at = pl.ds(2 * u, 2)
             for ab in range(2):
-                c = dot(wt[u], yret[n, ab, u]).reshape(2, T, w)
-                before = jnp.where(u == 3, 0.0, zbuf[n, ab, at].astype(F32))
+                c = dot(wt[u], yret[n, ab, u].reshape(ROWS, w)).reshape(2, T, w)
+                before = jnp.where(u == 0, 0.0, zbuf[n, ab, at].astype(F32))
                 zbuf[n, ab, at] = (before + c).astype(BF16)
 
         @pl.when(u == U - 1)
         def _():
             for ab in range(2):
-                c = dot(wtt[...], yret[n, ab, u]).reshape(NZ, T, w)
-                zbuf[n, ab, 0:6] = c[0:6].astype(BF16)
-                zbuf[n, ab, 6:8] = (zbuf[n, ab, 6:8].astype(F32) + c[6:8]).astype(BF16)
+                c = dot(wtt[...], yret[n, ab, u].reshape(ROWS, w)).reshape(NZ, T, w)
+                zbuf[n, ab, 0:2] = (zbuf[n, ab, 0:2].astype(F32) + c[0:2]).astype(BF16)
+                zbuf[n, ab, 2:8] = c[2:8].astype(BF16)
 
     def fcopy(n):
         return remote(fin_s.at[n], fin_r.at[n], fs.at[n], fr.at[n], xdev(1))
 
-    for n in range(4):
+    for n in range(C):
         zstart(n, 1)
+    build(0)
+
+    def first(n, _):
+        gather_half(n, 0)
+        ystart(yout, rows, ys4.at[n], yr4.at[n], yl4.at[n], n, 0, 1, 0)
+        return 0
+
+    lax.fori_loop(0, C, first, 0)
 
     def step(i, _):
-        u, n = lax.div(i, C), lax.rem(i, C)
+        def out_at(i):
+            late = i - (U - 2) * C
+            u = jnp.where(late < 0, lax.div(i, C) + 1, jnp.where(late < C // 2, 0, U - 1))
+            return u, jnp.where(late < 0, lax.rem(i, C), jnp.where(late < C // 2, 2 * late, late - C // 2))
+
+        def on_out(i):
+            return pl.when(jnp.logical_and(i >= 0, i < S))
         j, k = i - LY, i - LX
-        ju, jn = lax.div(j, C), lax.rem(j, C)
-        ku, kn = lax.div(k, C), lax.rem(k, C)
-
-        @on(i)
-        def _():
-            for pair in range(4):
-                @pl.when(u == pair)
+        u, n = out_at(i)
+        ju, jn = out_at(j)
+        ku, kn = out_at(k)
+
+        @pl.when(i < C)
+        def _():
+            ywait(yout, rows, ys4.at[i], yr4.at[i], yl4.at[i], i, 0, 0)
+            for way in range(2):
+                xcopy(i, 0, way, 0).start()
+
+        @on_out(i)
+        def _():
+            for h in range(1, 4):
+                @pl.when(u == h)
                 def _():
-                    zwait(n, pair + 1)
-                    if pair < 3:
-                        zstart(n, pair + 2)
+                    zwait(n, h)
+                    zstart(n, h + 1)
 
                     @pl.when(n == 0)
                     def _():
-                        build(pair)
-            gather(n, u)
-            ystart(yout, rows, ys, yr, yl, n, u, 1)
+                        build(POS[h])
+                        build(POS[NZ - h])
+
+            @pl.when(u == 0)
+            def _():
+                for m in range(2):
+                    zwait(n + m, 4)
+                    if m == 0:
+                        @pl.when(n == 0)
+                        def _():
+                            build(POS[4])
+                    gather_half(n + m, 1)
+                    ystart(yout, rows, ys.at[n + m, 0], yr.at[n + m, 0], yl.at[n + m, 0], n + m, 0, 1, 1)
+
+            @pl.when(u > 0)
+            def _():
+                gather(n, u)
+                ystart(yout, rows, ys.at[n, u], yr.at[n, u], yl.at[n, u], n, u, 1)
 
         @pl.when(i == LY)
         def _():
             w_copies[0].wait()
             w_copies[1].wait()
 
-        @on(j)
-        def _():
-            ywait(yout, rows, ys, yr, yl, jn, ju)
-            for way in range(2):
-                xcopy(jn, ju, way).start()
-            up_to(jn, ju, 0)
-
-        @on(k)
-        def _():
-            for way in range(2):
-                xcopy(kn, ku, way).wait_recv()
-            up_to(kn, ku, 2)
-
-            @pl.when(kn == C - 1)
-            def _():
-                activate(ku)
+        @on_out(j)
+        def _():
+            @pl.when(ju == 0)
+            def _():
+                for m in range(2):
+                    ywait(yout, rows, ys.at[jn + m, 0], yr.at[jn + m, 0], yl.at[jn + m, 0], jn + m, 0, 1)
+                    for way in range(2):
+                        xcopy(jn + m, 0, way, 1).start()
+                    up_to(jn + m, 0, 0)
+
+            @pl.when(ju > 0)
+            def _():
+                ywait(yout, rows, ys.at[jn, ju], yr.at[jn, ju], yl.at[jn, ju], jn, ju)
+                for way in range(2):
+                    xcopy(jn, ju, way).start()
+                up_to(jn, ju, 0)
+
+        @on_out(k)
+        def _():
+            @pl.when(ku == 0)
+            def _():
+                for m in range(2):
+                    for b in range(2):
+                        for way in range(2):
+                            xcopy(kn + m, 0, way, b).wait_recv()
+                    up_to(kn + m, 0, 2)
+
+                @pl.when(kn == C - 2)
+                def _():
+                    activate(0)
+
+            @pl.when(ku > 0)
+            def _():
+                for way in range(2):
+                    xcopy(kn, ku, way).wait_recv()
+                up_to(kn, ku, 2)
+
+                @pl.when(kn == C - 1)
+                def _():
+                    activate(ku)
 
         r = i - R0
         rj, rk = r - KX, r - KY
 
         def unit(q):
-            return jnp.where(q == 0, 3, jnp.where(q == 1, 4, 4 - q))
+            return jnp.where(q == 0, 0, U - q)
         ru, rn = unit(lax.div(r, C)), lax.rem(r, C)
         rju, rjn = unit(lax.div(rj, C)), lax.rem(rj, C)
         rku, rkn = unit(lax.div(rk, C)), lax.rem(rk, C)
@@ -289,30 +372,47 @@
 
         @on(r)
         def _():
-            ysent(yout, rows, ys, yr, rn, ru)
+            @pl.when(ru == 0)
+            def _():
+                yall(yout, rows, ys4.at[rn], yr4.at[rn], rn, 0, 0).wait_send()
+                yall(yout, rows, ys.at[rn, 0], yr.at[rn, 0], rn, 0, 1).wait_send()
+
+            @pl.when(ru > 0)
+            def _():
+                yall(yout, rows, ys.at[rn, ru], yr.at[rn, ru], rn, ru).wait_send()
             for way in range(2):
-                yout[rn, way, ru] = down(rn, ru, 2 + way).astype(BF16)
+                yout[rn, way, ru] = down(rn, ru, 2 + way).astype(BF16).reshape(NP, B, w)
                 x2copy(rn, ru, way).start()
 
         @on(rj)
         def _():
+            @pl.when(rju == 0)
+            def _():
+                for ab in range(2):
+                    for b in range(2):
+                        xcopy(rjn, 0, ab, b).wait_send()
+
+            @pl.when(rju > 0)
+            def _():
+                for ab in range(2):
+                    xcopy(rjn, rju, ab).wait_send()
             for ab in range(2):
-                xcopy(rjn, rju, ab).wait_send()
                 x2copy(rjn, rju, 1 - ab).wait_recv()
-                rows[rjn, ab, rju] = (down(rjn, rju, ab) + pxin[rjn, ab, rju].astype(F32)).astype(BF16)
-            ystart(rows, yret, ys2, yr2, yl2, rjn, rju, -1)
+                both = down(rjn, rju, ab) + pxin[rjn, ab, rju].reshape(ROWS, w).astype(F32)
+                rows[rjn, ab, rju] = both.astype(BF16).reshape(NP, B, w)
+            ystart(rows, yret, ys2.at[rjn, rju], yr2.at[rjn, rju], yl2.at[rjn, rju], rjn, rju, -1)
 
         @on(rk)
         def _():
-            ywait(rows, yret, ys2, yr2, yl2, rkn, rku)
-
-            @pl.when(rku == 3)
+            ywait(rows, yret, ys2.at[rkn, rku], yr2.at[rkn, rku], yl2.at[rkn, rku], rkn, rku)
+
+            @pl.when(rku == 0)
             def _():
                 for way in range(2):
                     for h in range(1, 5):
                         zcopy(rkn, way, h).wait_send()
             combine(rkn, rku)
-            for v, h in ((4, 1), (2, 2), (1, 3), (0, 4)):
+            for v, h in ((4, 1), (3, 2), (2, 3), (1, 4)):
                 @pl.when(rku == v)
                 def _():
                     if h > 1:
@@ -351,7 +451,7 @@
                 z2copy(n, way, h).wait_send()
 
         def unit(u, _):
-            ysent(rows, yret, ys2, yr2, n, u)
+            yall(rows, yret, ys2.at[n, u], yr2.at[n, u], n, u).wait_send()
             for way in range(2):
                 x2copy(n, u, way).wait_send()
             return 0
@@ -377,18 +477,19 @@
         scratch_shapes=[
             pltpu.VMEM((C, 2, NZ, T, w), BF16),
             pltpu.VMEM((NZ, 128, T), BF16),
-            pltpu.VMEM((U - 1, ROWS, 2 * T), BF16),
+            pltpu.VMEM((U - 2, ROWS, 2 * T), BF16),
             pltpu.VMEM((ROWS, NZ * T), BF16),
+            pltpu.VMEM((2, NP * HEAD, T), BF16),
             pltpu.VMEM((U - 1, 2 * T, ROWS), BF16),
             pltpu.VMEM((NZ * T, ROWS), BF16),
-            pltpu.VMEM((C, 2, U, ROWS, w), BF16),
-            pltpu.VMEM((C, 4, U, ROWS, w), BF16),
+            pltpu.VMEM((C, 2, U, NP, B, w), BF16),
+            pltpu.VMEM((C, 4, U, NP, B, w), BF16),
             pltpu.VMEM((U, ROWS, 2 * FF), F32),
             pltpu.VMEM((D, 2 * FF), BF16),
             pltpu.VMEM((FF, D), BF16),
             pltpu.VMEM((U, ROWS, FF), BF16),
-            pltpu.VMEM((C, 2, U, ROWS, w), BF16),
-            pltpu.VMEM((C, 2, U, ROWS, w), BF16),
+            pltpu.VMEM((C, 2, U, NP, B, w), BF16),
+            pltpu.VMEM((C, 2, U, NP, B, w), BF16),
             pltpu.VMEM((C, 2, 4, 2, T, w), BF16),
             pltpu.VMEM((C, T, w), F32),
             pltpu.VMEM((C, T, w), BF16),
@@ -400,6 +501,8 @@
             dma((C, U, 2)), dma((C, U, 2)),
             dma((C, 2, 4)), dma((C, 2, 4)),
             dma((C, U)), dma((C, U)), dma((C, U)),
+            dma((C,)), dma((C,)), dma((C,)),
+            dma((C, 2)), dma((C, 2)),
             dma((C, U, 2)), dma((C, U, 2)),
             dma((C,)), dma((C,)),
         ],

time: 161 us -> 155 us (0.963)
  Pallas kernels: 158 us -> 152 us
    pallas_call x1, Pallas kernels: 158 us -> 152 us  [local(): pl.pallas_call(kernel, out_shape=jax.ShapeDtypeStruct((T, D // NX), BF16)...]
where the time goes in v4:
time: 155 us; the launch traced here: 154 us
  Pallas kernels  152 us (98%)
  local copies, waits for them, and re-layouts  1.67 us (1%)
    pallas_call x1, Pallas kernels, local(): pl.pallas_call(kernel, out_shape=jax.ShapeDtypeStruct((T, D // NX), BF16)...  152 us

profile of v4, /device:TPU:8, one launch (start us, length us, event | category | flops | bytes accessed | tf_op | source)
XLA Modules:
  0.0 154.1 jit_solution(7332634322931720381)
XLA Ops:
  0.0 152.4 %shard_map.64 = bf16[128,1024]{1,0:T(8,128)(2,1)} custom-call(s32[8,128]{1,0:T(8,128)} %bitcast.2, f32[8,128]{1,0:T(8,128)} %bitcast.3, bf16[128,4096]{1,0:T(8,128)(2,1)} %tok.1, bf16[1,4096,384]{2,1,0:T(8,128)(2,1)} %wg_h.1, bf16[1,4096,384]{2,1,0:T(8,128)(2,1)} %wu_h.1, bf16[1,384,4096]{2,1,0:T(8,128)(2,1)} %wd_h.1), custom_call_target="tpu_custom_call" | custom-call | flops 16000000000 | bytes 11000000 | tf_op jit(solution)/shard_map/pallas_call | solution.py:472
  152.4 1.7 %copy.8 = bf16[128,1024]{1,0:T(8,128)(2,1)} copy(bf16[128,1024]{1,0:T(8,128)(2,1)} %shard_map.64) | data formatting | bytes 524288
